TPU v7x, 256 devices: a whole 4x4x8 slice. The times are simulated.
256 devices in a mesh: scan: 128 (over y_lo, z, x, core), det: 2 (over y_hi).
Axes of the slice: x: 4, y: 4 (y_hi: 2, y_lo: 2; y = y_hi * 2 + y_lo), z: 8, core: 2. Of those that a mesh axis runs over, the one named last changes fastest.
Arguments:
- frames: bfloat16 [512, 512, 1024], P('scan', None, 'det'), may hold values from -6 to 6
- exposure: float32 [512, 512], P('scan'), may hold values from 0.25 to 4
- dark_counts: int32 [1024, 1024], P('scan', 'det'), may hold values from 0 to 11, as said below
- aberration: float32 [1024], P('det'), may hold values from -3.140625 to 3.140625
- margin_codes: int32 [512, 512, 1024], P('scan', None, 'det'), may hold values from 0 to 2, as said below
Outputs:
- object_spectrum: float32 [2, 512, 512], P(None, 'scan', 'det')
Inputs may be any that keep to these rules, and one draw needn't show every extreme that they name: `dark_counts`: whole counts; their mean rises with the frame number. `margin_codes`: 1 marks the left double-margin region, 2 the right one, 0 neither; the code is 0 for every pixel at the frequency with q = 0 and a = 0.
All inputs are finite; a program needn't handle non-finite values.
Results may differ from a plain program's by a relative error of at most 0.008.
Values may be sent and summed in bfloat16 or wider, within the bound.
A program may use at most 64 MiB of HBM per device.

v0:
```python
import math

import jax
import jax.numpy as jnp
from jax import lax
from jax.sharding import PartitionSpec as P


def dft_tables(length):
    index_row = jnp.arange(length, dtype=jnp.int32)
    phase_table = (
        2.0
        * math.pi
        / length
        * (index_row[:, None] * index_row[None, :] % length).astype(jnp.float32)
    )
    norm_scale = 1.0 / math.sqrt(length)
    return (
        (jnp.cos(phase_table) * norm_scale).astype(jnp.bfloat16),
        (-jnp.sin(phase_table) * norm_scale).astype(jnp.bfloat16),
    )


def on_device(frames, exposure, dark_counts, aberration, margin_codes):
    scan_count = lax.axis_size("scan")
    det_count = lax.axis_size("det")
    local_sum = jnp.sum(dark_counts.astype(jnp.float32), axis=0)
    dark_mean = lax.psum(local_sum, "scan") / (dark_counts.shape[0] * scan_count)
    corrected = (
        frames.astype(jnp.float32) - exposure[:, :, None] * dark_mean[None, None, :]
    ).astype(jnp.bfloat16)
    cos_x, sin_x = dft_tables(frames.shape[1])
    cos_y, sin_y = dft_tables(frames.shape[0] * scan_count)
    pix_local = frames.shape[2]
    pix_total = pix_local * det_count
    phase_cos = jnp.cos(aberration)
    phase_sin = jnp.sin(aberration)
    weight = (margin_codes == 1).astype(jnp.float32) - (margin_codes == 2).astype(jnp.float32)
    spectra_real = jnp.einsum("yxp,xq->yqp", corrected, cos_x, preferred_element_type=jnp.float32)
    spectra_imag = jnp.einsum("yxp,xq->yqp", corrected, sin_x, preferred_element_type=jnp.float32)
    received = lax.all_to_all(
        jnp.stack([spectra_real, spectra_imag]).astype(jnp.bfloat16),
        "scan",
        split_axis=2,
        concat_axis=1,
        tiled=True,
    )
    full_real = jnp.einsum(
        "ay,yqp->qap", cos_y, received[0], preferred_element_type=jnp.float32
    ) - jnp.einsum("ay,yqp->qap", sin_y, received[1], preferred_element_type=jnp.float32)
    full_imag = jnp.einsum(
        "ay,yqp->qap", cos_y, received[1], preferred_element_type=jnp.float32
    ) + jnp.einsum("ay,yqp->qap", sin_y, received[0], preferred_element_type=jnp.float32)
    spectrum = jnp.stack([full_real, full_imag])
    part_real = jnp.sum(weight * (spectrum[0] * phase_cos + spectrum[1] * phase_sin), axis=2)
    part_imag = jnp.sum(weight * (spectrum[1] * phase_cos - spectrum[0] * phase_sin), axis=2)
    partial_value = jnp.stack([part_real, part_imag])
    return lax.psum_scatter(
        partial_value / math.sqrt(pix_total), "det", scatter_dimension=2, tiled=True
    )


def solution(mesh):
    placed = (
        P("scan", None, "det"),
        P("scan", None),
        P("scan", "det"),
        P("det"),
        P("scan", None, "det"),
    )
    return jax.shard_map(
        on_device, mesh=mesh, in_specs=placed, out_specs=P(None, "scan", "det"), check_vma=False
    )
```

profile of v0, /device:TPU:1, one launch (start us, length us, event | category | flops | bytes accessed | tf_op | source)
XLA Modules:
  0.0 484.4 jit_solution(3219898407658746270)
XLA Ops:
  6.5 0.7 convert_reduce_fusion
  7.3 279.7 %psum.7 = f32[512]{0:T(512)S(1)} all-reduce(f32[512]{0:T(512)S(1)} %convert_reduce_fusion), channel_id=1, replica_groups=mesh['scan'=128,'det'=2] {'scan'}, use_global_device_ids=true, to_apply=%region_1.0 | all-reduce | flops 512 | bytes 4096 | tf_op jit(solution)/shard_map/psum | solution.py:28
  286.9 0.0 copy-start.4
  286.9 0.0 copy-start.5
  286.9 6.9 %convert_bitcast_fusion = bf16[1,4,512,512]{3,2,1,0:T(8,128)(2,1)S(1)} fusion(bf16[4,512,512]{2,1,0:T(8,128)(2,1)} %param.5, f32[512]{0:T(512)S(1)} %broadcast_multiply_fusion, f32[4,512]{1,0:T(4,128)} %param.6), kind=kOutput, calls=%fused_computation.10 | convolution fusion | flops 1083441152 | bytes 4204544 | tf_op jit(solution)/shard_map/yxp,xq->yqp/dot_general | solution.py:40
  293.8 0.0 copy-done.4
  293.8 0.0 copy-done.5
  293.9 5.1 %convert_bitcast_fusion.1 = bf16[1,4,512,512]{3,2,1,0:T(8,128)(2,1)S(1)} fusion(bf16[4,512,512]{2,1,0:T(8,128)(2,1)S(1)} %copy-done.4, f32[512]{0:T(512)S(1)} %broadcast_multiply_fusion, f32[4,512]{1,0:T(4,128)S(1)} %copy-done.5), kind=kOutput, calls=%fused_computation.11 | convolution fusion | flops 1083179008 | bytes 4204544 | tf_op jit(solution)/shard_map/yxp,xq->yqp/dot_general | solution.py:39
  299.0 0.4 pad_maximum_fusion
  299.4 5.6 %copy.25 = bf16[2,4,512,512]{3,1,0,2:T(4,128)(2,1)} copy(bf16[2,4,512,512]{3,2,1,0:T(8,128)(2,1)S(1)} %pad_maximum_fusion) | data formatting | bytes 8388608 | tf_op jit(solution)/shard_map/stack | solution.py:42
  305.0 12.2 %all-to-all-start = ((bf16[2,4,512,512]{3,1,0,2:T(4,128)(2,1)}), bf16[2,4,512,512]{3,1,0,2:T(4,128)(2,1)}, u32[]{:S(2)}, u32[]{:S(2)}) async-start(bf16[2,4,512,512]{3,1,0,2:T(4,128)(2,1)} %copy.25), calls=%async_computation | async-start | bytes 8388608 | tf_op jit(solution)/shard_map/all_to_all | solution.py:41
  317.2 0.0 copy-start.3
  317.2 0.0 reduce-scatter.4.cloned.1.call-start
  317.3 5.3 %copy.21 = s32[4,512,512]{1,2,0:T(8,128)} copy(s32[4,512,512]{2,1,0:T(8,128)} %param.9) | data formatting | bytes 8388608 | tf_op args[4]
  322.5 0.0 copy-done.3
  322.6 4.3 broadcast_compare_fusion.1
  326.9 88.2 %all-to-all-done = bf16[2,4,512,512]{3,1,0,2:T(4,128)(2,1)} async-done(((bf16[2,4,512,512]{3,1,0,2:T(4,128)(2,1)}), bf16[2,4,512,512]{3,1,0,2:T(4,128)(2,1)}, u32[]{:S(2)}, u32[]{:S(2)}) %all-to-all-start) | async-done | bytes 4194336 | tf_op jit(solution)/shard_map/all_to_all | solution.py:41
  415.1 5.4 %copy.38 = bf16[2,4,128,4,512]{4,3,1,2,0:T(4,128)(2,1)S(1)} copy(bf16[2,4,128,4,512]{4,1,0,3,2:T(4,128)(2,1)} %bitcast.6) | data formatting | bytes 8388608 | tf_op jit(solution)/shard_map/all_to_all | solution.py:41
  420.5 3.1 fusion.48
  423.6 3.0 copy.27
  426.6 8.2 %fusion.15 = f32[4,512,512]{2,1,0:T(8,128)} fusion(bf16[512,4,512]{0,2,1:T(8,128)(2,1)} %copy.27), kind=kOutput, calls=%fused_computation.28 | convolution fusion | flops 1077936128 | bytes 6291456 | tf_op jit(solution)/shard_map/ay,yqp->qap/dot_general | solution.py:48
  434.8 3.0 copy.28
  437.8 0.0 copy-start
  437.8 7.5 %fusion.13 = f32[4,512,512]{2,1,0:T(8,128)S(1)} fusion(bf16[512,4,512]{0,2,1:T(8,128)(2,1)S(1)} %copy.28), kind=kOutput, calls=%fused_computation.27 | convolution fusion | flops 1077936128 | bytes 6291456 | tf_op jit(solution)/shard_map/ay,yqp->qap/dot_general | solution.py:51
  445.3 0.0 copy-done
  445.3 0.0 copy-start.1
  445.3 0.0 copy-start.2
  445.3 8.2 %convolution_subtract_fusion = f32[4,512,512]{2,1,0:T(8,128)S(1)} fusion(f32[4,512,512]{2,1,0:T(8,128)S(1)} %copy-done, bf16[512,4,512]{0,2,1:T(8,128)(2,1)S(1)} %copy.28), kind=kOutput, calls=%fused_computation.9 | convolution fusion | flops 1079246848 | bytes 10485760 | tf_op jit(solution)/shard_map/ay,yqp->qap/dot_general | solution.py:50
  453.5 0.0 copy-done.1
  453.5 0.0 copy-done.2
  453.5 7.3 %fusion.1 = (f32[4,512]{1,0:T(4,128)S(1)}, f32[4,512]{1,0:T(4,128)S(1)}) fusion(f32[4,512,512]{2,1,0:T(8,128)S(1)} %convolution_subtract_fusion, pred[4,512,512]{1,2,0:T(32,128)(4,1)S(1)} %copy-done.2, pred[4,512,512]{1,2,0:T(32,128)(4,1)S(1)} %get-tuple-element.7, f32[512]{0:T(512)S(1)} %get-tuple-element.12, f32[512]{0:T(512)S(1)} %get-tuple-element.11, ...), kind=kOutput, calls=%fused_computation.4 | convolution fusion | flops 1092874240 | bytes 12603392 | tf_op jit(solution)/shard_map/ay,yqp->qap/dot_general | solution.py:53
  460.8 0.3 copy.35
  461.1 1.0 reshape.12
  462.1 0.0 reduce-scatter.4.cloned.1.call-update
  462.1 13.4 %reduce-scatter.4.cloned.1.call-done = f32[256,8]{1,0:T(8,128)} async-done(((f32[512,8]{1,0:T(8,128)}), f32[256,8]{1,0:T(8,128)}) %reduce-scatter.4.cloned.1.call-update) | async-done | bytes 8208
  475.5 1.1 reshape.13
  476.6 0.7 copy.36
  (3 shorter events, 0.1 us)
Async XLA Ops:
  286.9 6.9 %copy-start.4 = (bf16[4,512,512]{2,1,0:T(8,128)(2,1)S(1)}, bf16[4,512,512]{2,1,0:T(8,128)(2,1)}, u32[]{:S(2)}) copy-start(bf16[4,512,512]{2,1,0:T(8,128)(2,1)} %param.5) | copy-start | bytes 6291460
  286.9 6.9 %copy-start.5 = (f32[4,512]{1,0:T(4,128)S(1)}, f32[4,512]{1,0:T(4,128)}, u32[]{:S(2)}) copy-start(f32[4,512]{1,0:T(4,128)} %param.6) | copy-start | bytes 24580
  305.0 110.1 %all-to-all-start = ((bf16[2,4,512,512]{3,1,0,2:T(4,128)(2,1)}), bf16[2,4,512,512]{3,1,0,2:T(4,128)(2,1)}, u32[]{:S(2)}, u32[]{:S(2)}) async-start(bf16[2,4,512,512]{3,1,0,2:T(4,128)(2,1)} %copy.25), calls=%async_computation | async-start | bytes 8388608 | tf_op jit(solution)/shard_map/all_to_all | solution.py:41
  317.2 5.3 %copy-start.3 = (f32[512]{0:T(512)S(1)}, f32[512]{0:T(512)}, u32[]{:S(2)}) copy-start(f32[512]{0:T(512)} %param.8) | copy-start | bytes 6148
  317.2 158.3 %reduce-scatter.4.cloned.1.call-start = ((), (), s32[]{:S(2)}) async-start(), calls=%async_computation.2 | async-start | bytes 393216
  437.8 7.5 %copy-start = (f32[4,512,512]{2,1,0:T(8,128)S(1)}, f32[4,512,512]{2,1,0:T(8,128)}, u32[]{:S(2)}) copy-start(f32[4,512,512]{2,1,0:T(8,128)} %fusion.15) | copy-start | bytes 12582916
  445.3 8.2 %copy-start.1 = (bf16[512,4,512]{0,2,1:T(8,128)(2,1)S(1)}, bf16[512,4,512]{0,2,1:T(8,128)(2,1)}, u32[]{:S(2)}) copy-start(bf16[512,4,512]{0,2,1:T(8,128)(2,1)} %copy.27) | copy-start | bytes 6291460
  445.3 8.2 %copy-start.2 = (pred[4,512,512]{1,2,0:T(32,128)(4,1)S(1)}, pred[4,512,512]{1,2,0:T(32,128)(4,1)}, u32[]{:S(2)}) copy-start(pred[4,512,512]{1,2,0:T(32,128)(4,1)} %get-tuple-element.8) | copy-start | bytes 3145732
Sparse Core Ops, SparseCore 0:
  462.2 13.2 reduce-scatter.3
where the time goes:
time: 494 us; the launch traced here: 484 us
  blocking collectives  280 us (57%)
  waiting for transfers between devices  102 us (21%)
  matrix products  43.1 us (9%)
  local copies, waits for them, and re-layouts  28.5 us (6%)
  between operations  13.7 us (3%)
  starting transfers between devices  12.3 us (2%)
  other arithmetic  5.44 us (1%)
    psum x1, blocking collectives, on_device(): lax.psum(local_sum, 'scan') / (dark_counts.shape[0] * scan_count)  280 us
    all_to_all x1, waiting for transfers between devices, on_device(): lax.all_to_all(jnp.stack([spectra_real, spectra_imag]).astype(jnp.bfloat1...  88.2 us
    unnamed x2, waiting for transfers between devices  13.5 us
    all_to_all x1, starting transfers between devices, on_device(): lax.all_to_all(jnp.stack([spectra_real, spectra_imag]).astype(jnp.bfloat1...  12.2 us
  transfers between devices with their start and end apart: 2, of which 2 were waited for; matrix products, arithmetic and copies ran while one was open for 2% of the time, Pallas kernels for 0%

commit v1 on v0

v1 whole, which is shorter than its diff:
```python
import functools
import math

import jax
import jax.numpy as jnp
import ml_dtypes
import numpy as np
from jax import lax
from jax.experimental import pallas as pl
from jax.experimental.pallas import tpu as pltpu
from jax.sharding import PartitionSpec as P

MESH = pl.DeviceIdType.MESH
LANES = 128
NEAR = 8


def dft_tables(length):
    index_row = np.arange(length, dtype=np.int64)
    products = (index_row[:, None] * index_row[None, :] % length).astype(np.float32)
    phase = np.float32(2.0 * math.pi / length) * products
    scale = np.float32(1.0 / math.sqrt(length))
    return (
        (np.cos(phase) * scale).astype(ml_dtypes.bfloat16),
        (-np.sin(phase) * scale).astype(ml_dtypes.bfloat16),
    )


def row_table(length):
    cos, sin = dft_tables(length)
    return np.stack([cos.T, sin.T], axis=1).reshape(2 * length, length)


def column_table(length, rows, tile):
    cos, sin = dft_tables(length)
    real = np.stack([cos, -sin], axis=1)
    imag = np.stack([sin, cos], axis=1)
    both = np.stack([real, imag]).reshape(2, length, 2, length // rows, rows)
    both = both.transpose(0, 1, 3, 2, 4).reshape(2, length // tile, tile, 2 * length)
    return np.ascontiguousarray(both.transpose(1, 0, 2, 3)).reshape(
        length // tile, 2 * tile, 2 * length
    )


def kernel(
    n, rows, chunks, tile, frame_total, scale,
    frames, exposure, dark, aberration, codes, row_tab, col_tab, out,
    frames_v, codes_v, row_v, col_v, spread, corrected, wide, send, recv, gathered, acc,
    near_buf, far_buf, dark_row, turn, halves, half_in,
    load_sem, near_sem, far_sem, send_sem, recv_sem, det_sem,
):
    me = lax.axis_index("scan")
    det = lax.axis_index("det")
    nx = frames_v.shape[2]
    q_rows = 2 * rows * rows
    far = n // NEAR

    loads = [pltpu.make_async_copy(row_tab, row_v, load_sem.at[0])]
    loads += [
        pltpu.make_async_copy(
            frames.at[:, :, pl.ds(c * LANES, LANES)], frames_v.at[c], load_sem.at[1 + c]
        )
        for c in range(chunks)
    ]
    loads.append(pltpu.make_async_copy(col_tab, col_v, load_sem.at[1 + chunks]))
    code_loads = [
        pltpu.make_async_copy(
            codes.at[:, :, pl.ds(c * LANES, LANES)], codes_v.at[c], load_sem.at[2 + chunks + c]
        )
        for c in range(chunks)
    ]
    for load in loads + code_loads:
        load.start()

    barrier = pltpu.get_barrier_semaphore()

    def greet(j, carry):
        pl.semaphore_signal(
            barrier, inc=1, device_id={"scan": lax.rem(me + j, n)}, device_id_type=MESH
        )
        return carry

    lax.fori_loop(1, n, greet, 0)
    pl.semaphore_signal(barrier, inc=1, device_id={"det": 1 - det}, device_id_type=MESH)

    position = lax.rem(me, NEAR)
    group = me // NEAR
    local_sum = jnp.sum(dark[...].astype(jnp.float32), axis=0, keepdims=True)
    near_buf[position] = local_sum
    turned = jnp.concatenate([exposure[...], jnp.zeros_like(exposure[...])], axis=0).T
    for y in range(rows):
        spread[y] = jnp.broadcast_to(turned[:, y : y + 1], (nx, LANES))
    angle = jnp.broadcast_to(aberration[...], (8, aberration.shape[1]))
    cos, sin = jnp.cos(angle), jnp.sin(angle)
    for c in range(chunks):
        turn[c, 0] = cos[:, c * LANES : (c + 1) * LANES]
        turn[c, 1] = sin[:, c * LANES : (c + 1) * LANES]
    acc[...] = jnp.zeros_like(acc)

    pl.semaphore_wait(barrier, n)

    def send_near(j, carry):
        peer = group * NEAR + lax.rem(position + j, NEAR)
        pltpu.make_async_remote_copy(
            src_ref=near_buf.at[position], dst_ref=near_buf.at[position],
            send_sem=near_sem.at[0], recv_sem=near_sem.at[1],
            device_id={"scan": peer}, device_id_type=MESH,
        ).start()
        return carry

    lax.fori_loop(1, NEAR, send_near, 0)
    some = near_buf.at[pl.ds(0, NEAR - 1)]
    pltpu.make_async_copy(some, some, near_sem.at[1]).wait()
    far_buf[group] = jnp.sum(near_buf[...], axis=0)

    def send_far(j, carry):
        peer = lax.rem(group + j, far) * NEAR + position
        pltpu.make_async_remote_copy(
            src_ref=far_buf.at[group], dst_ref=far_buf.at[group],
            send_sem=far_sem.at[0], recv_sem=far_sem.at[1],
            device_id={"scan": peer}, device_id_type=MESH,
        ).start()
        return carry

    lax.fori_loop(1, far, send_far, 0)
    most = far_buf.at[pl.ds(0, far - 1)]
    pltpu.make_async_copy(most, most, far_sem.at[1]).wait()
    mean = jnp.sum(far_buf[...], axis=0) / frame_total
    for c in range(chunks):
        dark_row[c] = jnp.broadcast_to(mean[:, c * LANES : (c + 1) * LANES], (8, LANES))

    loads[0].wait()
    m_tile = 512

    def spectra(c, carry):
        pltpu.make_async_copy(frames_v.at[c], frames_v.at[c], load_sem.at[1 + c]).wait()
        level = jnp.broadcast_to(dark_row[c, 0:1], (nx, LANES))
        for y in range(rows):
            value = frames_v[c, y].astype(jnp.float32) - spread[y] * level
            corrected[:, y * LANES : (y + 1) * LANES] = value.astype(jnp.bfloat16)
        for m in range(2 * nx // m_tile):
            part = jnp.dot(
                row_v[m * m_tile : (m + 1) * m_tile], corrected[...],
                preferred_element_type=jnp.float32,
            )
            for y in range(rows):
                wide[pl.ds(m * m_tile * rows + y, m_tile, stride=rows), :] = part[
                    :, y * LANES : (y + 1) * LANES
                ]

        def narrow(i, carry):
            at = pl.multiple_of(i * 512, 512)
            send[c, pl.ds(at, 512)] = wide[pl.ds(at, 512)].astype(jnp.bfloat16)
            return carry

        lax.fori_loop(0, n * q_rows // 512, narrow, 0)

        def ship(j, carry):
            peer = lax.rem(me + j, n)
            pltpu.make_async_remote_copy(
                src_ref=send.at[c, pl.ds(pl.multiple_of(peer * q_rows, q_rows), q_rows)],
                dst_ref=recv.at[c, pl.ds(pl.multiple_of(me * q_rows, q_rows), q_rows)],
                send_sem=send_sem, recv_sem=recv_sem.at[c],
                device_id={"scan": peer}, device_id_type=MESH,
            ).start()
            return carry

        lax.fori_loop(1, n, ship, 0)
        mine = pl.ds(pl.multiple_of(me * q_rows, q_rows), q_rows)
        recv[c, mine] = send[c, mine]
        return carry

    lax.fori_loop(0, chunks, spectra, 0)

    loads[1 + chunks].wait()

    def weigh(c, carry):
        pltpu.make_async_copy(codes_v.at[c], codes_v.at[c], load_sem.at[2 + chunks + c]).wait()
        others = recv.at[c, pl.ds(0, (n - 1) * q_rows)]
        pltpu.make_async_copy(others, others, recv_sem.at[c]).wait()

        def regroup(s, carry):
            at = pl.multiple_of(s * 2 * q_rows, 2 * q_rows)
            block = recv[c, pl.ds(at, 2 * q_rows)].astype(jnp.float32)
            unit = 2 * rows
            to = pl.ds(pl.multiple_of(s * 2 * unit, 2 * unit), 2 * unit)
            for q in range(rows):
                pair = jnp.concatenate(
                    [
                        block[q * unit : (q + 1) * unit],
                        block[q_rows + q * unit : q_rows + (q + 1) * unit],
                    ],
                    axis=0,
                )
                gathered[to, q * LANES : (q + 1) * LANES] = pair.astype(jnp.bfloat16)
            return carry

        lax.fori_loop(0, n // 2, regroup, 0, unroll=4)
        cos = jnp.broadcast_to(turn[c, 0, 0:1], (tile, LANES))
        sin = jnp.broadcast_to(turn[c, 1, 0:1], (tile, LANES))

        def column(t, carry):
            full = jnp.dot(col_v[t], gathered[...], preferred_element_type=jnp.float32)
            at = pl.ds(pl.multiple_of(t * tile, tile), tile)
            for q in range(rows):
                real = full[:tile, q * LANES : (q + 1) * LANES]
                imag = full[tile:, q * LANES : (q + 1) * LANES]
                code = codes_v[c, q, at]
                weight = (code == 1).astype(jnp.float32) - (code == 2).astype(jnp.float32)
                acc[q, at] += weight * (real * cos + imag * sin)
                acc[rows + q, at] += weight * (imag * cos - real * sin)
            return carry

        lax.fori_loop(0, col_v.shape[0], column, 0)
        return carry

    lax.fori_loop(0, chunks, weigh, 0)

    row = lax.broadcasted_iota(jnp.int32, (2 * rows, LANES), 0)
    total = jnp.zeros((2 * rows, acc.shape[1]), jnp.float32)
    for i in range(2 * rows):
        pick = (row == i).astype(jnp.bfloat16)
        value = acc[i]
        for _ in range(3):
            high = value.astype(jnp.bfloat16)
            total += lax.dot_general(
                pick, high, (((1,), (1,)), ((), ())), preferred_element_type=jnp.float32
            )
            value = value - high.astype(jnp.float32)
    total = total / scale
    width = half_in.shape[1]
    halves[0] = total[:, :width]
    halves[1] = total[:, width:]
    swap = pltpu.make_async_remote_copy(
        src_ref=halves.at[1 - det], dst_ref=half_in, send_sem=det_sem.at[0],
        recv_sem=det_sem.at[1], device_id={"det": 1 - det}, device_id_type=MESH,
    )
    swap.start()
    swap.wait()
    result = halves[det] + half_in[...]
    out[0] = result[:rows]
    out[1] = result[rows:]

    pltpu.make_async_copy(some, some, near_sem.at[0]).wait()
    pltpu.make_async_copy(most, most, far_sem.at[0]).wait()
    sent = send.at[:, pl.ds(0, (n - 1) * q_rows)]
    pltpu.make_async_copy(sent, sent, send_sem).wait()


def solution(mesh):
    n = mesh.shape["scan"]

    def on_device(frames, exposure, dark_counts, aberration, margin_codes):
        rows, nx, pix = frames.shape
        ny = rows * n
        chunks = pix // LANES
        tile = 256
        row_tab = row_table(nx)
        col_tab = column_table(ny, rows, tile)
        hbm = pl.BlockSpec(memory_space=pl.ANY)
        vmem = pl.BlockSpec(memory_space=pltpu.VMEM)
        body = functools.partial(
            kernel, n, rows, chunks, tile, dark_counts.shape[0] * n,
            math.sqrt(pix * mesh.shape["det"]),
        )
        message_rows = 2 * rows * ny
        return pl.pallas_call(
            body,
            out_shape=jax.ShapeDtypeStruct((2, rows, ny // mesh.shape["det"]), jnp.float32),
            in_specs=[hbm, vmem, vmem, vmem, hbm, hbm, hbm],
            out_specs=vmem,
            scratch_shapes=[
                pltpu.VMEM((chunks, rows, nx, LANES), jnp.bfloat16),
                pltpu.VMEM((chunks, rows, ny, LANES), jnp.int32),
                pltpu.VMEM(row_tab.shape, jnp.bfloat16),
                pltpu.VMEM(col_tab.shape, jnp.bfloat16),
                pltpu.VMEM((rows, nx, LANES), jnp.float32),
                pltpu.VMEM((nx, rows * LANES), jnp.bfloat16),
                pltpu.VMEM((message_rows, LANES), jnp.float32),
                pltpu.VMEM((chunks, message_rows, LANES), jnp.bfloat16),
                pltpu.VMEM((chunks, message_rows, LANES), jnp.bfloat16),
                pltpu.VMEM((2 * ny, rows * LANES), jnp.bfloat16),
                pltpu.VMEM((2 * rows, ny, LANES), jnp.float32),
                pltpu.VMEM((NEAR, 1, pix), jnp.float32),
                pltpu.VMEM((n // NEAR, 1, pix), jnp.float32),
                pltpu.VMEM((chunks, 8, LANES), jnp.float32),
                pltpu.VMEM((chunks, 2, 8, LANES), jnp.float32),
                pltpu.VMEM((2, 2 * rows, ny // 2), jnp.float32),
                pltpu.VMEM((2 * rows, ny // 2), jnp.float32),
                pltpu.SemaphoreType.DMA((2 + 2 * chunks,)),
                pltpu.SemaphoreType.DMA((2,)),
                pltpu.SemaphoreType.DMA((2,)),
                pltpu.SemaphoreType.DMA,
                pltpu.SemaphoreType.DMA((chunks,)),
                pltpu.SemaphoreType.DMA((2,)),
            ],
            compiler_params=pltpu.CompilerParams(
                collective_id=0, has_side_effects=True, vmem_limit_bytes=52 * 1024 * 1024
            ),
        )(
            frames, exposure, dark_counts, aberration.reshape(1, pix), margin_codes,
            jnp.asarray(row_tab), jnp.asarray(col_tab),
        )

    placed = (
        P("scan", None, "det"),
        P("scan", None),
        P("scan", "det"),
        P("det"),
        P("scan", None, "det"),
    )
    return jax.shard_map(
        on_device, mesh=mesh, in_specs=placed, out_specs=P(None, "scan", "det"), check_vma=False
    )
```

time: 494 us -> 125 us (0.25); the launches traced: 484 us -> 125 us
  blocking collectives: 280 us -> 0 us
  Pallas kernels: 0 us -> 121 us
  waiting for transfers between devices: 102 us -> 0 us
  matrix products: 43.1 us -> 0 us
  local copies, waits for them, and re-layouts: 28.5 us -> 3.92 us
  between operations: 13.7 us -> 0.01 us
  starting transfers between devices: 12.3 us -> 0 us
  other arithmetic: 5.44 us -> 0 us
    psum x1 -> x0, blocking collectives: 280 us -> none  [on_device(): lax.psum(local_sum, 'scan') / (dark_counts.shape[0] * scan_count)]
    pallas_call x0 -> x1, Pallas kernels: none -> 121 us  [on_device(): pl.pallas_call(body, out_shape=jax.ShapeDtypeStruct((2, rows, ny // mesh....]
    all_to_all x1 -> x0, waiting for transfers between devices: 88.2 us -> none  [on_device(): lax.all_to_all(jnp.stack([spectra_real, spectra_imag]).astype(jnp.bfloat1...]
    dot_general x6 -> x0, matrix products: 43.1 us -> none  [the longest x1 8.21 us: on_device(): jnp.einsum('ay,yqp->qap', cos_y, received[0], preferred_element_type=jnp....]
    unnamed x2 -> x0, waiting for transfers between devices: 13.5 us -> none
    all_to_all x1 -> x0, starting transfers between devices: 12.2 us -> none  [on_device(): lax.all_to_all(jnp.stack([spectra_real, spectra_imag]).astype(jnp.bfloat1...]
    squeeze x2 -> x0, local copies, waits for them, and re-layouts: 5.97 us -> none  [the longest x1 3.01 us: on_device(): received[0]]
    another operation x1 -> x0, local copies, waits for them, and re-layouts: 5.61 us -> none  [on_device(): jnp.stack([spectra_real, spectra_imag]).astype(jnp.bfloat16)]
  transfers between devices with their start and end apart: 2 -> 0, of which waited for: 2 -> 0; matrix products, arithmetic and copies ran while one was open for 2% -> 0% of each run, Pallas kernels for 0% -> 0%
where the time goes in v1:
time: 125 us
  Pallas kernels  121 us (97%)
  local copies, waits for them, and re-layouts  3.92 us (3%)
    pallas_call x1, Pallas kernels, on_device(): pl.pallas_call(body, out_shape=jax.ShapeDtypeStruct((2, rows, ny // mesh....  121 us
    unnamed x9, local copies, waits for them, and re-layouts  3.92 us

profile of v1, /device:TPU:1, one launch (start us, length us, event | category | flops | bytes accessed | tf_op | source)
XLA Modules:
  0.0 125.0 jit_solution(17502854189488146484)
XLA Ops:
  0.0 0.0 copy-start
  0.0 1.2 copy-done
  1.2 0.0 copy-start.1
  1.2 0.7 copy-done.1
  1.9 0.0 copy-start.2
  1.9 0.7 copy-done.2
  2.6 0.0 copy-start.3
  2.6 0.7 copy-done.3
  3.3 121.1 %shard_map.73 = f32[2,4,256]{2,1,0:T(4,128)S(1)} custom-call(bf16[4,512,512]{2,1,0:T(8,128)(2,1)} %frames.1, f32[4,512]{1,0:T(4,128)S(1)} %copy-done.2, s32[8,512]{1,0:T(8,128)S(1)} %copy-done.1, f32[1,512]{1,0:T(1,128)S(1)} %bitcast.1, s32[4,512,512]{2,1,0:T(8,128)} %codes.1, bf16[1024,512]{1,0:T(8,128)(2,1)S(1)} %copy-done, ...), custom_call_target="tpu_custom_call" | custom-call | tf_op jit(solution)/shard_map/pallas_call | solution.py:267
  124.4 0.6 copy.9
Async XLA Ops:
  0.0 1.2 copy-start
  1.2 0.7 copy-start.1
  1.9 0.7 copy-start.2
  2.6 0.7 copy-start.3

commit v2 on v1

--- a/solution.py
+++ b/solution.py
@@ -44,10 +44,11 @@
 
 def kernel(
     n, rows, chunks, tile, frame_total, scale,
-    frames, exposure, dark, aberration, codes, row_tab, col_tab, out,
-    frames_v, codes_v, row_v, col_v, spread, corrected, wide, send, recv, gathered, acc,
-    near_buf, far_buf, dark_row, turn, halves, half_in,
-    load_sem, near_sem, far_sem, send_sem, recv_sem, det_sem,
+    frames, exposure_h, dark_h, aberration_h, codes, row_tab, col_tab, out,
+    exposure, dark, aberration,
+    frames_v, codes_v, row_v, col_v, joined, wide, level, send, recv, gathered, acc,
+    near_buf, far_buf, dark_row, turn, level_out, level_in, halves, half_in,
+    small_sem, load_sem, near_sem, far_sem, level_sem, send_sem, recv_sem, det_sem,
 ):
     me = lax.axis_index("scan")
     det = lax.axis_index("det")
@@ -55,6 +56,22 @@
     q_rows = 2 * rows * rows
     far = n // NEAR
 
+    barrier = pltpu.get_barrier_semaphore()
+
+    def greet(j, carry):
+        pl.semaphore_signal(
+            barrier, inc=1, device_id={"scan": lax.rem(me + j, n)}, device_id_type=MESH
+        )
+        return carry
+
+    lax.fori_loop(1, n, greet, 0)
+    pl.semaphore_signal(barrier, inc=1, device_id={"det": 1 - det}, device_id_type=MESH)
+
+    small = [
+        pltpu.make_async_copy(dark_h, dark, small_sem.at[0]),
+        pltpu.make_async_copy(exposure_h, exposure, small_sem.at[1]),
+        pltpu.make_async_copy(aberration_h, aberration, small_sem.at[2]),
+    ]
     loads = [pltpu.make_async_copy(row_tab, row_v, load_sem.at[0])]
     loads += [
         pltpu.make_async_copy(
@@ -69,78 +86,23 @@
         )
         for c in range(chunks)
     ]
-    for load in loads + code_loads:
+    for load in small + loads + code_loads:
         load.start()
-
-    barrier = pltpu.get_barrier_semaphore()
-
-    def greet(j, carry):
-        pl.semaphore_signal(
-            barrier, inc=1, device_id={"scan": lax.rem(me + j, n)}, device_id_type=MESH
-        )
-        return carry
-
-    lax.fori_loop(1, n, greet, 0)
-    pl.semaphore_signal(barrier, inc=1, device_id={"det": 1 - det}, device_id_type=MESH)
 
     position = lax.rem(me, NEAR)
     group = me // NEAR
-    local_sum = jnp.sum(dark[...].astype(jnp.float32), axis=0, keepdims=True)
-    near_buf[position] = local_sum
-    turned = jnp.concatenate([exposure[...], jnp.zeros_like(exposure[...])], axis=0).T
-    for y in range(rows):
-        spread[y] = jnp.broadcast_to(turned[:, y : y + 1], (nx, LANES))
-    angle = jnp.broadcast_to(aberration[...], (8, aberration.shape[1]))
-    cos, sin = jnp.cos(angle), jnp.sin(angle)
-    for c in range(chunks):
-        turn[c, 0] = cos[:, c * LANES : (c + 1) * LANES]
-        turn[c, 1] = sin[:, c * LANES : (c + 1) * LANES]
-    acc[...] = jnp.zeros_like(acc)
-
-    pl.semaphore_wait(barrier, n)
-
-    def send_near(j, carry):
-        peer = group * NEAR + lax.rem(position + j, NEAR)
-        pltpu.make_async_remote_copy(
-            src_ref=near_buf.at[position], dst_ref=near_buf.at[position],
-            send_sem=near_sem.at[0], recv_sem=near_sem.at[1],
-            device_id={"scan": peer}, device_id_type=MESH,
-        ).start()
-        return carry
-
-    lax.fori_loop(1, NEAR, send_near, 0)
-    some = near_buf.at[pl.ds(0, NEAR - 1)]
-    pltpu.make_async_copy(some, some, near_sem.at[1]).wait()
-    far_buf[group] = jnp.sum(near_buf[...], axis=0)
-
-    def send_far(j, carry):
-        peer = lax.rem(group + j, far) * NEAR + position
-        pltpu.make_async_remote_copy(
-            src_ref=far_buf.at[group], dst_ref=far_buf.at[group],
-            send_sem=far_sem.at[0], recv_sem=far_sem.at[1],
-            device_id={"scan": peer}, device_id_type=MESH,
-        ).start()
-        return carry
-
-    lax.fori_loop(1, far, send_far, 0)
-    most = far_buf.at[pl.ds(0, far - 1)]
-    pltpu.make_async_copy(most, most, far_sem.at[1]).wait()
-    mean = jnp.sum(far_buf[...], axis=0) / frame_total
-    for c in range(chunks):
-        dark_row[c] = jnp.broadcast_to(mean[:, c * LANES : (c + 1) * LANES], (8, LANES))
-
+    small[0].wait()
+    near_buf[position] = jnp.sum(dark[...].astype(jnp.float32), axis=0, keepdims=True)
     loads[0].wait()
     m_tile = 512
 
-    def spectra(c, carry):
-        pltpu.make_async_copy(frames_v.at[c], frames_v.at[c], load_sem.at[1 + c]).wait()
-        level = jnp.broadcast_to(dark_row[c, 0:1], (nx, LANES))
+    def spectra(c):
+        loads[1 + c].wait()
         for y in range(rows):
-            value = frames_v[c, y].astype(jnp.float32) - spread[y] * level
-            corrected[:, y * LANES : (y + 1) * LANES] = value.astype(jnp.bfloat16)
+            joined[:, y * LANES : (y + 1) * LANES] = frames_v[c, y]
         for m in range(2 * nx // m_tile):
             part = jnp.dot(
-                row_v[m * m_tile : (m + 1) * m_tile], corrected[...],
+                row_v[m * m_tile : (m + 1) * m_tile], joined[...],
                 preferred_element_type=jnp.float32,
             )
             for y in range(rows):
@@ -154,8 +116,11 @@
             return carry
 
         lax.fori_loop(0, n * q_rows // 512, narrow, 0)
-
-        def ship(j, carry):
+        mine = pl.ds(pl.multiple_of(me * q_rows, q_rows), q_rows)
+        recv[c, mine] = send[c, mine]
+
+    def ship(c):
+        def one(j, carry):
             peer = lax.rem(me + j, n)
             pltpu.make_async_remote_copy(
                 src_ref=send.at[c, pl.ds(pl.multiple_of(peer * q_rows, q_rows), q_rows)],
@@ -165,12 +130,103 @@
             ).start()
             return carry
 
-        lax.fori_loop(1, n, ship, 0)
-        mine = pl.ds(pl.multiple_of(me * q_rows, q_rows), q_rows)
-        recv[c, mine] = send[c, mine]
-        return carry
-
-    lax.fori_loop(0, chunks, spectra, 0)
+        lax.fori_loop(1, n, one, 0)
+
+    spectra(0)
+    pl.semaphore_wait(barrier, n)
+
+    def send_near(j, carry):
+        peer = group * NEAR + lax.rem(position + j, NEAR)
+        pltpu.make_async_remote_copy(
+            src_ref=near_buf.at[position], dst_ref=near_buf.at[position],
+            send_sem=near_sem.at[0], recv_sem=near_sem.at[1],
+            device_id={"scan": peer}, device_id_type=MESH,
+        ).start()
+        return carry
+
+    lax.fori_loop(1, NEAR, send_near, 0)
+    ship(0)
+    spectra(1)
+    ship(1)
+
+    small[1].wait()
+    turned = jnp.concatenate([exposure[...], jnp.zeros_like(exposure[...])], axis=0).T
+    for y in range(rows):
+        rest = jnp.broadcast_to(turned[:, y : y + 1], (nx, LANES))
+        total = jnp.zeros((2 * nx, LANES), jnp.float32)
+        for _ in range(3):
+            high = rest.astype(jnp.bfloat16)
+            total += jnp.dot(row_v[...], high, preferred_element_type=jnp.float32)
+            rest = rest - high.astype(jnp.float32)
+        level[pl.ds(y, 2 * nx, stride=rows), :] = total
+    per_row = LANES // q_rows
+    diagonal = lax.broadcasted_iota(jnp.int32, (LANES, LANES), 0) == lax.broadcasted_iota(
+        jnp.int32, (LANES, LANES), 1
+    )
+
+    def pack(i, carry):
+        block = level[pl.ds(pl.multiple_of(i * LANES, LANES), LANES)]
+        level_out[i] = jnp.sum(jnp.where(diagonal, block, 0.0), axis=0, keepdims=True)
+        return carry
+
+    lax.fori_loop(0, n // per_row, pack, 0)
+
+    def send_level(j, carry):
+        peer = lax.rem(me + j, n)
+        pltpu.make_async_remote_copy(
+            src_ref=level_out.at[peer // per_row], dst_ref=level_in.at[me],
+            send_sem=level_sem.at[0], recv_sem=level_sem.at[1],
+            device_id={"scan": peer}, device_id_type=MESH,
+        ).start()
+        return carry
+
+    lax.fori_loop(1, n, send_level, 0)
+    level_in[me] = level_out[me // per_row]
+
+    some = near_buf.at[pl.ds(0, NEAR - 1)]
+    pltpu.make_async_copy(some, some, near_sem.at[1]).wait()
+    far_buf[group] = jnp.sum(near_buf[...], axis=0)
+
+    def send_far(j, carry):
+        peer = lax.rem(group + j, far) * NEAR + position
+        pltpu.make_async_remote_copy(
+            src_ref=far_buf.at[group], dst_ref=far_buf.at[group],
+            send_sem=far_sem.at[0], recv_sem=far_sem.at[1],
+            device_id={"scan": peer}, device_id_type=MESH,
+        ).start()
+        return carry
+
+    lax.fori_loop(1, far, send_far, 0)
+    for c in range(2, chunks):
+        spectra(c)
+        ship(c)
+
+    small[2].wait()
+    angle = jnp.broadcast_to(aberration[...], (8, aberration.shape[1]))
+    cos, sin = jnp.cos(angle), jnp.sin(angle)
+    for c in range(chunks):
+        turn[c, 0] = cos[:, c * LANES : (c + 1) * LANES]
+        turn[c, 1] = sin[:, c * LANES : (c + 1) * LANES]
+    acc[...] = jnp.zeros_like(acc)
+    levels = level_in.at[pl.ds(0, n - 1)]
+    pltpu.make_async_copy(levels, levels, level_sem.at[1]).wait()
+    wide[0:n] = level_in[...].reshape(n, LANES).T
+    own = wide[pl.ds(pl.multiple_of(lax.rem(me, per_row) * q_rows, q_rows), q_rows)]
+    lane = lax.broadcasted_iota(jnp.int32, (q_rows, LANES), 1)
+
+    def unpack(s, carry):
+        column = jnp.sum(jnp.where(lane == s, own, 0.0), axis=1, keepdims=True)
+        level[pl.ds(pl.multiple_of(s * q_rows, q_rows), q_rows)] = jnp.broadcast_to(
+            column, (q_rows, LANES)
+        )
+        return carry
+
+    lax.fori_loop(0, n, unpack, 0)
+    most = far_buf.at[pl.ds(0, far - 1)]
+    pltpu.make_async_copy(most, most, far_sem.at[1]).wait()
+    mean = jnp.sum(far_buf[...], axis=0) / frame_total
+    for c in range(chunks):
+        dark_row[c] = jnp.broadcast_to(mean[:, c * LANES : (c + 1) * LANES], (8, LANES))
 
     loads[1 + chunks].wait()
 
@@ -179,9 +235,12 @@
         others = recv.at[c, pl.ds(0, (n - 1) * q_rows)]
         pltpu.make_async_copy(others, others, recv_sem.at[c]).wait()
 
+        dark_mean = jnp.broadcast_to(dark_row[c, 0:1], (2 * q_rows, LANES))
+
         def regroup(s, carry):
             at = pl.multiple_of(s * 2 * q_rows, 2 * q_rows)
             block = recv[c, pl.ds(at, 2 * q_rows)].astype(jnp.float32)
+            block = block - level[pl.ds(at, 2 * q_rows)] * dark_mean
             unit = 2 * rows
             to = pl.ds(pl.multiple_of(s * 2 * unit, 2 * unit), 2 * unit)
             for q in range(rows):
@@ -221,7 +280,7 @@
     for i in range(2 * rows):
         pick = (row == i).astype(jnp.bfloat16)
         value = acc[i]
-        for _ in range(3):
+        for _ in range(2):
             high = value.astype(jnp.bfloat16)
             total += lax.dot_general(
                 pick, high, (((1,), (1,)), ((), ())), preferred_element_type=jnp.float32
@@ -243,6 +302,7 @@
 
     pltpu.make_async_copy(some, some, near_sem.at[0]).wait()
     pltpu.make_async_copy(most, most, far_sem.at[0]).wait()
+    pltpu.make_async_copy(levels, levels, level_sem.at[0]).wait()
     sent = send.at[:, pl.ds(0, (n - 1) * q_rows)]
     pltpu.make_async_copy(sent, sent, send_sem).wait()
 
@@ -267,15 +327,18 @@
         return pl.pallas_call(
             body,
             out_shape=jax.ShapeDtypeStruct((2, rows, ny // mesh.shape["det"]), jnp.float32),
-            in_specs=[hbm, vmem, vmem, vmem, hbm, hbm, hbm],
+            in_specs=[hbm] * 7,
             out_specs=vmem,
             scratch_shapes=[
+                pltpu.VMEM((rows, nx), jnp.float32),
+                pltpu.VMEM(dark_counts.shape, jnp.int32),
+                pltpu.VMEM((1, pix), jnp.float32),
                 pltpu.VMEM((chunks, rows, nx, LANES), jnp.bfloat16),
                 pltpu.VMEM((chunks, rows, ny, LANES), jnp.int32),
                 pltpu.VMEM(row_tab.shape, jnp.bfloat16),
                 pltpu.VMEM(col_tab.shape, jnp.bfloat16),
-                pltpu.VMEM((rows, nx, LANES), jnp.float32),
                 pltpu.VMEM((nx, rows * LANES), jnp.bfloat16),
+                pltpu.VMEM((message_rows, LANES), jnp.float32),
                 pltpu.VMEM((message_rows, LANES), jnp.float32),
                 pltpu.VMEM((chunks, message_rows, LANES), jnp.bfloat16),
                 pltpu.VMEM((chunks, message_rows, LANES), jnp.bfloat16),
@@ -285,9 +348,13 @@
                 pltpu.VMEM((n // NEAR, 1, pix), jnp.float32),
                 pltpu.VMEM((chunks, 8, LANES), jnp.float32),
                 pltpu.VMEM((chunks, 2, 8, LANES), jnp.float32),
+                pltpu.VMEM((n * 2 * rows * rows // LANES, 1, LANES), jnp.float32),
+                pltpu.VMEM((n, 1, LANES), jnp.float32),
                 pltpu.VMEM((2, 2 * rows, ny // 2), jnp.float32),
                 pltpu.VMEM((2 * rows, ny // 2), jnp.float32),
+                pltpu.SemaphoreType.DMA((3,)),
                 pltpu.SemaphoreType.DMA((2 + 2 * chunks,)),
+                pltpu.SemaphoreType.DMA((2,)),
                 pltpu.SemaphoreType.DMA((2,)),
                 pltpu.SemaphoreType.DMA((2,)),
                 pltpu.SemaphoreType.DMA,
@@ -295,7 +362,7 @@
                 pltpu.SemaphoreType.DMA((2,)),
             ],
             compiler_params=pltpu.CompilerParams(
-                collective_id=0, has_side_effects=True, vmem_limit_bytes=52 * 1024 * 1024
+                collective_id=0, has_side_effects=True, vmem_limit_bytes=63 * 1024 * 1024
             ),
         )(
             frames, exposure, dark_counts, aberration.reshape(1, pix), margin_codes,

time: 125 us -> 116 us (0.928)
  Pallas kernels: 121 us -> 114 us
  local copies, waits for them, and re-layouts: 3.92 us -> 1.3 us
    pallas_call x1, Pallas kernels: 121 us -> 114 us  [on_device(): pl.pallas_call(body, out_shape=jax.ShapeDtypeStruct((2, rows, ny // mesh....]
    unnamed x9 -> x1, local copies, waits for them, and re-layouts: 3.92 us -> 1.3 us
where the time goes in v2:
time: 116 us
  Pallas kernels  114 us (98%)
  local copies, waits for them, and re-layouts  1.3 us (1%)
    pallas_call x1, Pallas kernels, on_device(): pl.pallas_call(body, out_shape=jax.ShapeDtypeStruct((2, rows, ny // mesh....  114 us

profile of v2, /device:TPU:1, one launch (start us, length us, event | category | flops | bytes accessed | tf_op | source)
XLA Modules:
  0.0 115.7 jit_solution(10889911609329490418)
XLA Ops:
  0.0 114.4 %shard_map.73 = f32[2,4,256]{2,1,0:T(4,128)} custom-call(bf16[4,512,512]{2,1,0:T(8,128)(2,1)} %frames.1, f32[4,512]{1,0:T(4,128)} %exposure_h.1, s32[8,512]{1,0:T(8,128)} %dark_h.1, f32[1,512]{1,0:T(1,128)} %bitcast.1, s32[4,512,512]{2,1,0:T(8,128)} %codes.1, bf16[1024,512]{1,0:T(8,128)(2,1)} %constant.4.clone.row_tab, ...), custom_call_target="tpu_custom_call" | custom-call | tf_op jit(solution)/shard_map/pallas_call | solution.py:327
  114.4 1.3 %copy.9 = f32[2,4,256]{2,1,0:T(4,128)} copy(f32[2,4,256]{2,1,0:T(4,128)} %shard_map.73) | data formatting | bytes 16384

commit v3 on v2

v3 whole, which is shorter than its diff:
```python
import functools
import math

import jax
import jax.numpy as jnp
import ml_dtypes
import numpy as np
from jax import lax
from jax.experimental import pallas as pl
from jax.experimental.pallas import tpu as pltpu
from jax.sharding import PartitionSpec as P

MESH = pl.DeviceIdType.MESH
LANES = 128
NEAR = 8


def dft_tables(length):
    index_row = np.arange(length, dtype=np.int64)
    products = (index_row[:, None] * index_row[None, :] % length).astype(np.float32)
    phase = np.float32(2.0 * math.pi / length) * products
    scale = np.float32(1.0 / math.sqrt(length))
    return (
        (np.cos(phase) * scale).astype(ml_dtypes.bfloat16),
        (-np.sin(phase) * scale).astype(ml_dtypes.bfloat16),
    )


def row_table(length):
    cos, sin = dft_tables(length)
    return np.stack([cos.T, sin.T], axis=1).reshape(2 * length, length)


def column_table(length, rows, tile):
    cos, sin = dft_tables(length)
    real = np.stack([cos, -sin], axis=1)
    imag = np.stack([sin, cos], axis=1)
    both = np.stack([real, imag]).reshape(2, length, 2, length // rows, rows)
    both = both.transpose(0, 1, 3, 2, 4).reshape(2, length // tile, tile, 2 * length)
    return np.ascontiguousarray(both.transpose(1, 0, 2, 3)).reshape(
        length // tile, 2 * tile, 2 * length
    )


def kernel(
    n, rows, chunks, tile, frame_total, scale,
    frames, exposure_h, dark_h, aberration_h, codes, row_tab, col_tab, out,
    exposure, dark, aberration,
    frames_v, codes_v, row_v, col_v, joined, wide, level, send, stage, recv, gathered, acc,
    near_buf, far_buf, dark_row, turn, level_out, level_stage, level_pack, level_in, halves, half_in,
    small_sem, load_sem, dark_near_sem, dark_far_sem, level_near_sem, level_far_sem,
    near_send, near_recv, far_send, far_recv, det_sem,
):
    me = lax.axis_index("scan")
    det = lax.axis_index("det")
    nx = frames_v.shape[2]
    unit = 2 * rows
    q_rows = unit * rows
    far = n // NEAR
    position = lax.rem(me, NEAR)
    group = lax.div(me, NEAR)

    def near_peer(j):
        return lax.rem(position + j, NEAR)

    def far_peer(j):
        return lax.rem(group + j, far)

    def at(g, p):
        return {"scan": g * NEAR + p}

    barrier = pltpu.get_barrier_semaphore()
    for j in range(1, far):
        pl.semaphore_signal(
            barrier, inc=1, device_id=at(far_peer(j), position), device_id_type=MESH
        )
    for j in range(1, NEAR):
        pl.semaphore_signal(barrier, inc=1, device_id=at(group, near_peer(j)), device_id_type=MESH)
    pl.semaphore_signal(barrier, inc=1, device_id={"det": 1 - det}, device_id_type=MESH)

    small = [
        pltpu.make_async_copy(dark_h, dark, small_sem.at[0]),
        pltpu.make_async_copy(exposure_h, exposure, small_sem.at[1]),
        pltpu.make_async_copy(aberration_h, aberration, small_sem.at[2]),
    ]
    loads = [pltpu.make_async_copy(row_tab, row_v, load_sem.at[0])]
    loads += [
        pltpu.make_async_copy(
            frames.at[:, :, pl.ds(c * LANES, LANES)], frames_v.at[c], load_sem.at[1 + c]
        )
        for c in range(chunks)
    ]
    loads.append(pltpu.make_async_copy(col_tab, col_v, load_sem.at[1 + chunks]))
    loads += [
        pltpu.make_async_copy(
            codes.at[:, :, pl.ds(c * LANES, LANES)], codes_v.at[c], load_sem.at[2 + chunks + c]
        )
        for c in range(chunks)
    ]
    first_loads = small + loads[: 1 + chunks]
    for load in first_loads:
        load.start()

    small[0].wait()
    near_buf[position] = jnp.sum(dark[...].astype(jnp.float32), axis=0, keepdims=True)
    loads[0].wait()
    m_tile = 512

    parts = []
    for c in range(chunks):
        count = rows // 2 if c in (0, chunks - 1) else rows
        parts += [(c, first, count) for first in range(0, rows, count)]

    def spectra(c):
        loads[1 + c].wait()
        for y in range(rows):
            joined[:, y * LANES : (y + 1) * LANES] = frames_v[c, y]
        for m in range(2 * nx // m_tile):
            part = jnp.dot(
                row_v[m * m_tile : (m + 1) * m_tile], joined[...],
                preferred_element_type=jnp.float32,
            )
            for y in range(rows):
                wide[pl.ds(m * m_tile * rows + y, m_tile, stride=rows), :] = part[
                    :, y * LANES : (y + 1) * LANES
                ]

        def narrow(g, carry):
            block = wide[pl.ds(pl.multiple_of(g * NEAR * q_rows, q_rows), NEAR * q_rows)]
            send[c, g] = block.astype(jnp.bfloat16).reshape(NEAR, q_rows, LANES)
            return carry

        lax.fori_loop(0, far, narrow, 0)
        recv[c, group, 0] = send[c, group, position]

    def ship_near(k):
        c, first, count = parts[k]
        span = pl.ds(first * unit, count * unit)
        for j in range(1, NEAR):
            peer = near_peer(j)
            pltpu.make_async_remote_copy(
                src_ref=send.at[c, :, peer, span], dst_ref=stage.at[c, :, NEAR - j, span],
                send_sem=near_send, recv_sem=near_recv.at[k],
                device_id=at(group, peer), device_id_type=MESH,
            ).start()

    def ship_own(k):
        c, first, count = parts[k]
        span = pl.ds(first * unit, count * unit)

        def one(j, carry):
            peer = far_peer(j)
            pltpu.make_async_remote_copy(
                src_ref=send.at[c, peer, position, span], dst_ref=recv.at[c, group, 0, span],
                send_sem=far_send, recv_sem=far_recv.at[k],
                device_id=at(peer, position), device_id_type=MESH,
            ).start()
            return carry

        lax.fori_loop(1, far, one, 0)

    def ship_far(k):
        c, first, count = parts[k]
        span = pl.ds(first * unit, count * unit)
        rest = pl.ds(1, NEAR - 1)

        def one(j, carry):
            peer = far_peer(j)
            pltpu.make_async_remote_copy(
                src_ref=stage.at[c, peer, rest, span], dst_ref=recv.at[c, group, rest, span],
                send_sem=far_send, recv_sem=far_recv.at[k],
                device_id=at(peer, position), device_id_type=MESH,
            ).start()
            return carry

        lax.fori_loop(1, far, one, 0)

    def arrive_near(k):
        c, first, count = parts[k]
        span = pl.ds(first * unit, count * unit)
        slots = stage.at[c, :, pl.ds(1, NEAR - 1), span]
        pltpu.make_async_copy(slots, slots, near_recv.at[k]).wait()
        recv[c, group, 1:, span] = stage[c, group, 1:, span]

    spectra(0)
    pl.semaphore_wait(barrier, NEAR + far - 1)

    ship_near(0)
    ship_own(0)
    ship_near(1)
    ship_own(1)
    for load in loads[1 + chunks :]:
        load.start()
    for j in range(1, NEAR):
        pltpu.make_async_remote_copy(
            src_ref=near_buf.at[position], dst_ref=near_buf.at[position],
            send_sem=dark_near_sem.at[0], recv_sem=dark_near_sem.at[1],
            device_id=at(group, near_peer(j)), device_id_type=MESH,
        ).start()
    for c in range(1, chunks):
        spectra(c)
        for k, part in enumerate(parts):
            if part[0] == c:
                ship_own(k)

    small[1].wait()
    turned = jnp.concatenate([exposure[...], jnp.zeros_like(exposure[...])], axis=0).T
    for y in range(rows):
        rest = jnp.broadcast_to(turned[:, y : y + 1], (nx, LANES))
        total = jnp.zeros((2 * nx, LANES), jnp.float32)
        for _ in range(3):
            high = rest.astype(jnp.bfloat16)
            total += jnp.dot(row_v[...], high, preferred_element_type=jnp.float32)
            rest = rest - high.astype(jnp.float32)
        wide[pl.ds(y, 2 * nx, stride=rows), :] = total
    per_row = LANES // q_rows
    per_group = NEAR // per_row
    diagonal = lax.broadcasted_iota(jnp.int32, (LANES, LANES), 0) == lax.broadcasted_iota(
        jnp.int32, (LANES, LANES), 1
    )

    def pack(g, carry):
        for h in range(per_group):
            start = pl.multiple_of((g * per_group + h) * LANES, LANES)
            row = jnp.where(diagonal, wide[pl.ds(start, LANES)], 0.0)
            level_out[h, pl.ds(g, 1)] = jnp.sum(row, axis=0, keepdims=True)
        return carry

    lax.fori_loop(0, far, pack, 0)
    half = lax.div(position, per_row)
    level_stage[0] = level_out[half]
    for j in range(1, NEAR):
        peer = near_peer(j)
        pltpu.make_async_remote_copy(
            src_ref=level_out.at[lax.div(peer, per_row)], dst_ref=level_stage.at[NEAR - j],
            send_sem=level_near_sem.at[0], recv_sem=level_near_sem.at[1],
            device_id=at(group, peer), device_id_type=MESH,
        ).start()
    for k in range(2, len(parts)):
        ship_near(k)

    arrive_near(0)
    ship_far(0)
    arrive_near(1)
    ship_far(1)

    near_some = near_buf.at[pl.ds(0, NEAR - 1)]
    pltpu.make_async_copy(near_some, near_some, dark_near_sem.at[1]).wait()
    far_buf[group] = jnp.sum(near_buf[...], axis=0)

    def send_dark(j, carry):
        pltpu.make_async_remote_copy(
            src_ref=far_buf.at[group], dst_ref=far_buf.at[group],
            send_sem=dark_far_sem.at[0], recv_sem=dark_far_sem.at[1],
            device_id=at(far_peer(j), position), device_id_type=MESH,
        ).start()
        return carry

    lax.fori_loop(1, far, send_dark, 0)


    level_near = level_stage.at[pl.ds(1, NEAR - 1)]
    pltpu.make_async_copy(level_near, level_near, level_near_sem.at[1]).wait()
    lane = lax.broadcasted_iota(jnp.int32, (far, LANES), 1)
    place = lax.rem(position, per_row)
    for h in range(per_group):
        row = jnp.zeros((far, LANES), jnp.float32)
        for m in range(per_row):
            block = jnp.where(lane // q_rows == place, level_stage[h * per_row + m], 0.0)
            row += pltpu.roll(block, lax.rem((m - place + per_row) * q_rows, LANES), axis=1)
        level_pack[h] = row.reshape(far, 1, LANES)
    level_in[:, group] = level_pack[:, group]

    def send_level(j, carry):
        peer = far_peer(j)
        pltpu.make_async_remote_copy(
            src_ref=level_pack.at[:, peer], dst_ref=level_in.at[:, group],
            send_sem=level_far_sem.at[0], recv_sem=level_far_sem.at[1],
            device_id=at(peer, position), device_id_type=MESH,
        ).start()
        return carry

    lax.fori_loop(1, far, send_level, 0)

    for k in range(2, len(parts)):
        arrive_near(k)
        ship_far(k)

    small[2].wait()
    angle = jnp.broadcast_to(aberration[...], (8, aberration.shape[1]))
    cos, sin = jnp.cos(angle), jnp.sin(angle)
    for c in range(chunks):
        turn[c, 0] = cos[:, c * LANES : (c + 1) * LANES]
        turn[c, 1] = sin[:, c * LANES : (c + 1) * LANES]
    acc[...] = jnp.zeros_like(acc)
    level_far = level_in.at[:, pl.ds(0, far - 1)]
    pltpu.make_async_copy(level_far, level_far, level_far_sem.at[1]).wait()
    columns = level_in[...].reshape(per_group * far, LANES).T
    index = lax.broadcasted_iota(jnp.int32, (q_rows, per_group * far), 1)

    def unpack(g, carry):
        for h in range(per_group):
            for m in range(per_row):
                block = jnp.where(index == h * far + g, columns[m * q_rows : (m + 1) * q_rows], 0.0)
                level[g, h * per_row + m] = jnp.broadcast_to(
                    jnp.sum(block, axis=1, keepdims=True), (q_rows, LANES)
                )
        return carry

    lax.fori_loop(0, far, unpack, 0)
    far_some = far_buf.at[pl.ds(0, far - 1)]
    pltpu.make_async_copy(far_some, far_some, dark_far_sem.at[1]).wait()
    mean = jnp.sum(far_buf[...], axis=0) / frame_total
    for c in range(chunks):
        dark_row[c] = jnp.broadcast_to(mean[:, c * LANES : (c + 1) * LANES], (8, LANES))

    loads[1 + chunks].wait()

    def weigh(k):
        c, first, count = parts[k]
        if first == 0:
            loads[2 + chunks + c].wait()
        span = pl.ds(first * unit, count * unit)
        others = recv.at[c, pl.ds(0, far - 1), :, span]
        pltpu.make_async_copy(others, others, far_recv.at[k]).wait()
        dark_mean = jnp.broadcast_to(dark_row[c, 0:1], (count * unit, LANES))

        def regroup(g, carry):
            for m in range(NEAR // 2):
                blocks = []
                for source in (2 * m, 2 * m + 1):
                    slot = lax.rem(source - position + NEAR, NEAR)
                    block = recv[c, g, slot, span].astype(jnp.float32)
                    blocks.append(block - level[g, slot, span] * dark_mean)
                to = pl.ds(pl.multiple_of((g * NEAR + 2 * m) * unit, 2 * unit), 2 * unit)
                for q in range(count):
                    pair = [block[q * unit : (q + 1) * unit] for block in blocks]
                    gathered[to, q * LANES : (q + 1) * LANES] = jnp.concatenate(
                        pair, axis=0
                    ).astype(jnp.bfloat16)
            return carry

        lax.fori_loop(0, far, regroup, 0)
        cos = jnp.broadcast_to(turn[c, 0, 0:1], (tile, LANES))
        sin = jnp.broadcast_to(turn[c, 1, 0:1], (tile, LANES))

        def column(t, carry):
            full = jnp.dot(
                col_v[t], gathered[:, : count * LANES], preferred_element_type=jnp.float32
            )
            here = pl.ds(pl.multiple_of(t * tile, tile), tile)
            for q in range(count):
                real = full[:tile, q * LANES : (q + 1) * LANES]
                imag = full[tile:, q * LANES : (q + 1) * LANES]
                code = codes_v[c, first + q, here]
                weight = (code == 1).astype(jnp.float32) - (code == 2).astype(jnp.float32)
                acc[first + q, here] += weight * (real * cos + imag * sin)
                acc[rows + first + q, here] += weight * (imag * cos - real * sin)
            return carry

        lax.fori_loop(0, col_v.shape[0], column, 0)

    for k in range(len(parts)):
        weigh(k)

    row = lax.broadcasted_iota(jnp.int32, (2 * rows, LANES), 0)
    total = jnp.zeros((2 * rows, acc.shape[1]), jnp.float32)
    for i in range(2 * rows):
        pick = (row == i).astype(jnp.bfloat16)
        value = acc[i]
        for _ in range(2):
            high = value.astype(jnp.bfloat16)
            total += lax.dot_general(
                pick, high, (((1,), (1,)), ((), ())), preferred_element_type=jnp.float32
            )
            value = value - high.astype(jnp.float32)
    total = total / scale
    width = half_in.shape[1]
    halves[0] = total[:, :width]
    halves[1] = total[:, width:]
    swap = pltpu.make_async_remote_copy(
        src_ref=halves.at[1 - det], dst_ref=half_in, send_sem=det_sem.at[0],
        recv_sem=det_sem.at[1], device_id={"det": 1 - det}, device_id_type=MESH,
    )
    swap.start()

    pltpu.make_async_copy(near_some, near_some, dark_near_sem.at[0]).wait()
    pltpu.make_async_copy(far_some, far_some, dark_far_sem.at[0]).wait()
    pltpu.make_async_copy(level_near, level_near, level_near_sem.at[0]).wait()
    pltpu.make_async_copy(level_far, level_far, level_far_sem.at[0]).wait()
    slots = stage.at[:, :, pl.ds(1, NEAR - 1)]
    pltpu.make_async_copy(slots, slots, near_send).wait()
    others = recv.at[:, pl.ds(0, far - 1)]
    pltpu.make_async_copy(others, others, far_send).wait()

    swap.wait()
    result = halves[det] + half_in[...]
    out[0] = result[:rows]
    out[1] = result[rows:]


def solution(mesh):
    n = mesh.shape["scan"]

    def on_device(frames, exposure, dark_counts, aberration, margin_codes):
        rows, nx, pix = frames.shape
        ny = rows * n
        chunks = pix // LANES
        tile = 256
        far = n // NEAR
        q_rows = 2 * rows * rows
        row_tab = row_table(nx)
        col_tab = column_table(ny, rows, tile)
        hbm = pl.BlockSpec(memory_space=pl.ANY)
        vmem = pl.BlockSpec(memory_space=pltpu.VMEM)
        body = functools.partial(
            kernel, n, rows, chunks, tile, dark_counts.shape[0] * n,
            math.sqrt(pix * mesh.shape["det"]),
        )
        spectra = pltpu.VMEM((chunks, far, NEAR, q_rows, LANES), jnp.bfloat16)
        packed = pltpu.VMEM((NEAR * q_rows // LANES, far, 1, LANES), jnp.float32)
        return pl.pallas_call(
            body,
            out_shape=jax.ShapeDtypeStruct((2, rows, ny // mesh.shape["det"]), jnp.float32),
            in_specs=[hbm] * 7,
            out_specs=vmem,
            scratch_shapes=[
                pltpu.VMEM((rows, nx), jnp.float32),
                pltpu.VMEM(dark_counts.shape, jnp.int32),
                pltpu.VMEM((1, pix), jnp.float32),
                pltpu.VMEM((chunks, rows, nx, LANES), jnp.bfloat16),
                pltpu.VMEM((chunks, rows, ny, LANES), jnp.int32),
                pltpu.VMEM(row_tab.shape, jnp.bfloat16),
                pltpu.VMEM(col_tab.shape, jnp.bfloat16),
                pltpu.VMEM((nx, rows * LANES), jnp.bfloat16),
                pltpu.VMEM((n * q_rows, LANES), jnp.float32),
                pltpu.VMEM((far, NEAR, q_rows, LANES), jnp.float32),
                spectra,
                spectra,
                spectra,
                pltpu.VMEM((2 * ny, rows * LANES), jnp.bfloat16),
                pltpu.VMEM((2 * rows, ny, LANES), jnp.float32),
                pltpu.VMEM((NEAR, 1, pix), jnp.float32),
                pltpu.VMEM((far, 1, pix), jnp.float32),
                pltpu.VMEM((chunks, 8, LANES), jnp.float32),
                pltpu.VMEM((chunks, 2, 8, LANES), jnp.float32),
                pltpu.VMEM((NEAR * q_rows // LANES, far, LANES), jnp.float32),
                pltpu.VMEM((NEAR, far, LANES), jnp.float32),
                packed,
                packed,
                pltpu.VMEM((2, 2 * rows, ny // 2), jnp.float32),
                pltpu.VMEM((2 * rows, ny // 2), jnp.float32),
                pltpu.SemaphoreType.DMA((3,)),
                pltpu.SemaphoreType.DMA((2 + 2 * chunks,)),
                pltpu.SemaphoreType.DMA((2,)),
                pltpu.SemaphoreType.DMA((2,)),
                pltpu.SemaphoreType.DMA((2,)),
                pltpu.SemaphoreType.DMA((2,)),
                pltpu.SemaphoreType.DMA,
                pltpu.SemaphoreType.DMA((chunks + 2,)),
                pltpu.SemaphoreType.DMA,
                pltpu.SemaphoreType.DMA((chunks + 2,)),
                pltpu.SemaphoreType.DMA((2,)),
            ],
            compiler_params=pltpu.CompilerParams(
                collective_id=0, has_side_effects=True, vmem_limit_bytes=63 * 1024 * 1024
            ),
        )(
            frames, exposure, dark_counts, aberration.reshape(1, pix), margin_codes,
            jnp.asarray(row_tab), jnp.asarray(col_tab),
        )

    placed = (
        P("scan", None, "det"),
        P("scan", None),
        P("scan", "det"),
        P("det"),
        P("scan", None, "det"),
    )
    return jax.shard_map(
        on_device, mesh=mesh, in_specs=placed, out_specs=P(None, "scan", "det"), check_vma=False
    )
```

time: 116 us -> 111 us (0.957)
  Pallas kernels: 114 us -> 110 us
    pallas_call x1, Pallas kernels: 114 us -> 110 us  [on_device(): pl.pallas_call(body, out_shape=jax.ShapeDtypeStruct((2, rows, ny // mesh....]
where the time goes in v3:
time: 111 us
  Pallas kernels  110 us (99%)
  local copies, waits for them, and re-layouts  1.3 us (1%)
    pallas_call x1, Pallas kernels, on_device(): pl.pallas_call(body, out_shape=jax.ShapeDtypeStruct((2, rows, ny // mesh....  110 us

profile of v3, /device:TPU:1, one launch (start us, length us, event | category | flops | bytes accessed | tf_op | source)
XLA Modules:
  0.0 110.9 jit_solution(8197609938933329183)
XLA Ops:
  0.0 109.6 %shard_map.73 = f32[2,4,256]{2,1,0:T(4,128)} custom-call(bf16[4,512,512]{2,1,0:T(8,128)(2,1)} %frames.1, f32[4,512]{1,0:T(4,128)} %exposure_h.1, s32[8,512]{1,0:T(8,128)} %dark_h.1, f32[1,512]{1,0:T(1,128)} %bitcast.1, s32[4,512,512]{2,1,0:T(8,128)} %codes.1, bf16[1024,512]{1,0:T(8,128)(2,1)} %constant.4.clone.row_tab, ...), custom_call_target="tpu_custom_call" | custom-call | tf_op jit(solution)/shard_map/pallas_call | solution.py:422
  109.6 1.3 %copy.9 = f32[2,4,256]{2,1,0:T(4,128)} copy(f32[2,4,256]{2,1,0:T(4,128)} %shard_map.73) | data formatting | bytes 16384

commit v4 on v3

--- a/solution.py
+++ b/solution.py
@@ -63,8 +63,14 @@
     def near_peer(j):
         return lax.rem(position + j, NEAR)
 
+    cross = (group >> 2) & 1
+
     def far_peer(j):
-        return lax.rem(group + j, far)
+        step = jnp.int32(j) - 1
+        first = step < 7 + cross
+        high = jnp.where(first, cross, 1 - cross)
+        base = jnp.where(first, step + 1 - cross, step - 7)
+        return group ^ ((base & 3) | ((base & 4) << 1) | (high << 2))
 
     def at(g, p):
         return {"scan": g * NEAR + p}

time: 111 us -> 110 us (level)
  no operation moved by 1% of the time
where the time goes in v4:
time: 110 us
  Pallas kernels  109 us (99%)
  local copies, waits for them, and re-layouts  1.3 us (1%)
    pallas_call x1, Pallas kernels, on_device(): pl.pallas_call(body, out_shape=jax.ShapeDtypeStruct((2, rows, ny // mesh....  109 us

profile of v4, /device:TPU:1, one launch (start us, length us, event | category | flops | bytes accessed | tf_op | source)
XLA Modules:
  0.0 110.3 jit_solution(8103786628997027417)
XLA Ops:
  0.0 109.0 %shard_map.73 = f32[2,4,256]{2,1,0:T(4,128)} custom-call(bf16[4,512,512]{2,1,0:T(8,128)(2,1)} %frames.1, f32[4,512]{1,0:T(4,128)} %exposure_h.1, s32[8,512]{1,0:T(8,128)} %dark_h.1, f32[1,512]{1,0:T(1,128)} %bitcast.1, s32[4,512,512]{2,1,0:T(8,128)} %codes.1, bf16[1024,512]{1,0:T(8,128)(2,1)} %constant.4.clone.row_tab, ...), custom_call_target="tpu_custom_call" | custom-call | tf_op jit(solution)/shard_map/pallas_call | solution.py:428
  109.0 1.3 %copy.9 = f32[2,4,256]{2,1,0:T(4,128)} copy(f32[2,4,256]{2,1,0:T(4,128)} %shard_map.73) | data formatting | bytes 16384

commit v5 on v4

--- a/solution.py
+++ b/solution.py
@@ -48,7 +48,7 @@
     exposure, dark, aberration,
     frames_v, codes_v, row_v, col_v, joined, wide, level, send, stage, recv, gathered, acc,
     near_buf, far_buf, dark_row, turn, level_out, level_stage, level_pack, level_in, halves, half_in,
-    small_sem, load_sem, dark_near_sem, dark_far_sem, level_near_sem, level_far_sem,
+    small_sem, load_sem, dark_near_sem, dark_far_sem, dark_row_sem, level_near_sem, level_far_sem,
     near_send, near_recv, far_send, far_recv, det_sem,
 ):
     me = lax.axis_index("scan")
@@ -108,7 +108,9 @@
         load.start()
 
     small[0].wait()
-    near_buf[position] = jnp.sum(dark[...].astype(jnp.float32), axis=0, keepdims=True)
+    counted = jnp.sum(dark[...].astype(jnp.float32), axis=0, keepdims=True)
+    for c in range(chunks):
+        near_buf[c, position] = counted[:, c * LANES : (c + 1) * LANES]
     loads[0].wait()
     m_tile = 512
 
@@ -199,7 +201,7 @@
         load.start()
     for j in range(1, NEAR):
         pltpu.make_async_remote_copy(
-            src_ref=near_buf.at[position], dst_ref=near_buf.at[position],
+            src_ref=near_buf.at[:, position], dst_ref=near_buf.at[:, position],
             send_sem=dark_near_sem.at[0], recv_sem=dark_near_sem.at[1],
             device_id=at(group, near_peer(j)), device_id_type=MESH,
         ).start()
@@ -250,9 +252,9 @@
     arrive_near(1)
     ship_far(1)
 
-    near_some = near_buf.at[pl.ds(0, NEAR - 1)]
+    near_some = near_buf.at[:, pl.ds(0, NEAR - 1)]
     pltpu.make_async_copy(near_some, near_some, dark_near_sem.at[1]).wait()
-    far_buf[group] = jnp.sum(near_buf[...], axis=0)
+    far_buf[group] = jnp.sum(near_buf[lax.rem(position, chunks)], axis=0)
 
     def send_dark(j, carry):
         pltpu.make_async_remote_copy(
@@ -316,9 +318,15 @@
     lax.fori_loop(0, far, unpack, 0)
     far_some = far_buf.at[pl.ds(0, far - 1)]
     pltpu.make_async_copy(far_some, far_some, dark_far_sem.at[1]).wait()
-    mean = jnp.sum(far_buf[...], axis=0) / frame_total
-    for c in range(chunks):
-        dark_row[c] = jnp.broadcast_to(mean[:, c * LANES : (c + 1) * LANES], (8, LANES))
+    dark_row[position] = jnp.sum(far_buf[...], axis=0) / frame_total
+    for j in range(1, NEAR):
+        pltpu.make_async_remote_copy(
+            src_ref=dark_row.at[position], dst_ref=dark_row.at[position],
+            send_sem=dark_row_sem.at[0], recv_sem=dark_row_sem.at[1],
+            device_id=at(group, near_peer(j)), device_id_type=MESH,
+        ).start()
+    rows_some = dark_row.at[pl.ds(0, NEAR - 1)]
+    pltpu.make_async_copy(rows_some, rows_some, dark_row_sem.at[1]).wait()
 
     loads[1 + chunks].wait()
 
@@ -329,7 +337,7 @@
         span = pl.ds(first * unit, count * unit)
         others = recv.at[c, pl.ds(0, far - 1), :, span]
         pltpu.make_async_copy(others, others, far_recv.at[k]).wait()
-        dark_mean = jnp.broadcast_to(dark_row[c, 0:1], (count * unit, LANES))
+        dark_mean = jnp.broadcast_to(dark_row[c], (count * unit, LANES))
 
         def regroup(g, carry):
             for m in range(NEAR // 2):
@@ -366,20 +374,25 @@
 
         lax.fori_loop(0, col_v.shape[0], column, 0)
 
-    for k in range(len(parts)):
+    row = lax.broadcasted_iota(jnp.int32, (2 * rows, LANES), 0)
+
+    def lane_sum(total, first, count):
+        for i in [p * rows + first + q for p in range(2) for q in range(count)]:
+            pick = (row == i).astype(jnp.bfloat16)
+            value = acc[i]
+            for _ in range(2):
+                high = value.astype(jnp.bfloat16)
+                total += lax.dot_general(
+                    pick, high, (((1,), (1,)), ((), ())), preferred_element_type=jnp.float32
+                )
+                value = value - high.astype(jnp.float32)
+        return total
+
+    total = jnp.zeros((2 * rows, acc.shape[1]), jnp.float32)
+    for k, (c, first, count) in enumerate(parts):
         weigh(k)
-
-    row = lax.broadcasted_iota(jnp.int32, (2 * rows, LANES), 0)
-    total = jnp.zeros((2 * rows, acc.shape[1]), jnp.float32)
-    for i in range(2 * rows):
-        pick = (row == i).astype(jnp.bfloat16)
-        value = acc[i]
-        for _ in range(2):
-            high = value.astype(jnp.bfloat16)
-            total += lax.dot_general(
-                pick, high, (((1,), (1,)), ((), ())), preferred_element_type=jnp.float32
-            )
-            value = value - high.astype(jnp.float32)
+        if c == chunks - 1:
+            total = lane_sum(total, first, count)
     total = total / scale
     width = half_in.shape[1]
     halves[0] = total[:, :width]
@@ -391,6 +404,7 @@
     swap.start()
 
     pltpu.make_async_copy(near_some, near_some, dark_near_sem.at[0]).wait()
+    pltpu.make_async_copy(rows_some, rows_some, dark_row_sem.at[0]).wait()
     pltpu.make_async_copy(far_some, far_some, dark_far_sem.at[0]).wait()
     pltpu.make_async_copy(level_near, level_near, level_near_sem.at[0]).wait()
     pltpu.make_async_copy(level_far, level_far, level_far_sem.at[0]).wait()
@@ -446,9 +460,9 @@
                 spectra,
                 pltpu.VMEM((2 * ny, rows * LANES), jnp.bfloat16),
                 pltpu.VMEM((2 * rows, ny, LANES), jnp.float32),
-                pltpu.VMEM((NEAR, 1, pix), jnp.float32),
-                pltpu.VMEM((far, 1, pix), jnp.float32),
-                pltpu.VMEM((chunks, 8, LANES), jnp.float32),
+                pltpu.VMEM((chunks, NEAR, 1, LANES), jnp.float32),
+                pltpu.VMEM((far, 1, LANES), jnp.float32),
+                pltpu.VMEM((NEAR, 1, LANES), jnp.float32),
                 pltpu.VMEM((chunks, 2, 8, LANES), jnp.float32),
                 pltpu.VMEM((NEAR * q_rows // LANES, far, LANES), jnp.float32),
                 pltpu.VMEM((NEAR, far, LANES), jnp.float32),
@@ -458,6 +472,7 @@
                 pltpu.VMEM((2 * rows, ny // 2), jnp.float32),
                 pltpu.SemaphoreType.DMA((3,)),
                 pltpu.SemaphoreType.DMA((2 + 2 * chunks,)),
+                pltpu.SemaphoreType.DMA((2,)),
                 pltpu.SemaphoreType.DMA((2,)),
                 pltpu.SemaphoreType.DMA((2,)),
                 pltpu.SemaphoreType.DMA((2,)),

time: 110 us -> 110 us (level)
  no operation moved by 1% of the time
where the time goes in v5:
time: 110 us
  Pallas kernels  108 us (98%)
  local copies, waits for them, and re-layouts  1.3 us (1%)
    pallas_call x1, Pallas kernels, on_device(): pl.pallas_call(body, out_shape=jax.ShapeDtypeStruct((2, rows, ny // mesh....  108 us

profile of v5, /device:TPU:1, one launch (start us, length us, event | category | flops | bytes accessed | tf_op | source)
XLA Modules:
  0.0 109.5 jit_solution(15705505034513872008)
XLA Ops:
  0.0 108.2 %shard_map.73 = f32[2,4,256]{2,1,0:T(4,128)} custom-call(bf16[4,512,512]{2,1,0:T(8,128)(2,1)} %frames.1, f32[4,512]{1,0:T(4,128)} %exposure_h.1, s32[8,512]{1,0:T(8,128)} %dark_h.1, f32[1,512]{1,0:T(1,128)} %bitcast.1, s32[4,512,512]{2,1,0:T(8,128)} %codes.1, bf16[1024,512]{1,0:T(8,128)(2,1)} %constant.4.clone.row_tab, ...), custom_call_target="tpu_custom_call" | custom-call | tf_op jit(solution)/shard_map/pallas_call | solution.py:442
  108.2 1.3 %copy.9 = f32[2,4,256]{2,1,0:T(4,128)} copy(f32[2,4,256]{2,1,0:T(4,128)} %shard_map.73) | data formatting | bytes 16384

commit v6 on v5

--- a/solution.py
+++ b/solution.py
@@ -116,7 +116,7 @@
 
     parts = []
     for c in range(chunks):
-        count = rows // 2 if c in (0, chunks - 1) else rows
+        count = rows // 2
         parts += [(c, first, count) for first in range(0, rows, count)]
 
     def spectra(c):
@@ -478,9 +478,9 @@
                 pltpu.SemaphoreType.DMA((2,)),
                 pltpu.SemaphoreType.DMA((2,)),
                 pltpu.SemaphoreType.DMA,
-                pltpu.SemaphoreType.DMA((chunks + 2,)),
+                pltpu.SemaphoreType.DMA((2 * chunks,)),
                 pltpu.SemaphoreType.DMA,
-                pltpu.SemaphoreType.DMA((chunks + 2,)),
+                pltpu.SemaphoreType.DMA((2 * chunks,)),
                 pltpu.SemaphoreType.DMA((2,)),
             ],
             compiler_params=pltpu.CompilerParams(

time: 110 us -> 110 us (level)
  no operation moved by 1% of the time
where the time goes in v6:
time: 110 us
  Pallas kernels  108 us (98%)
  local copies, waits for them, and re-layouts  1.3 us (1%)
    pallas_call x1, Pallas kernels, on_device(): pl.pallas_call(body, out_shape=jax.ShapeDtypeStruct((2, rows, ny // mesh....  108 us

profile of v6, /device:TPU:1, one launch (start us, length us, event | category | flops | bytes accessed | tf_op | source)
XLA Modules:
  0.0 109.5 jit_solution(4068384558090783737)
XLA Ops:
  0.0 108.2 %shard_map.73 = f32[2,4,256]{2,1,0:T(4,128)} custom-call(bf16[4,512,512]{2,1,0:T(8,128)(2,1)} %frames.1, f32[4,512]{1,0:T(4,128)} %exposure_h.1, s32[8,512]{1,0:T(8,128)} %dark_h.1, f32[1,512]{1,0:T(1,128)} %bitcast.1, s32[4,512,512]{2,1,0:T(8,128)} %codes.1, bf16[1024,512]{1,0:T(8,128)(2,1)} %constant.4.clone.row_tab, ...), custom_call_target="tpu_custom_call" | custom-call | tf_op jit(solution)/shard_map/pallas_call | solution.py:442
  108.2 1.3 %copy.9 = f32[2,4,256]{2,1,0:T(4,128)} copy(f32[2,4,256]{2,1,0:T(4,128)} %shard_map.73) | data formatting | bytes 16384
